TPU v7x, 32 devices: a whole 2x2x4 slice. The times are simulated.
32 devices in a mesh: groups: 2 (over y), seq: 16 (over z, x, core).
Axes of the slice: x: 2, y: 2, z: 4, core: 2. Of those that a mesh axis runs over, the one named last changes fastest.
Arguments:
- tokens: bfloat16 [8192, 256], P(('groups', 'seq')), parts along dimension 0, may hold values from -6 to 6
- norm_gain: float32 [256], replicated, may hold values from 0.1 to 1.9
- in_weight: bfloat16 [256, 768], replicated, may hold values from -0.375 to 0.375
- short_filter: float32 [3, 768], replicated, may hold values from -3 to 3
- spectra: bfloat16 [2, 256, 32, 256], P(None, None, 'seq'), may hold values from -6 to 6
- skip_gain: float32 [256], replicated, may hold values from -1 to 1
- out_weight: bfloat16 [256, 256], replicated, may hold values from -0.375 to 0.375
- mlp_gain: float32 [256], replicated, may hold values from 0.1 to 1.9
- up_weight: bfloat16 [256, 1024], replicated, may hold values from -0.375 to 0.375
- down_weight: bfloat16 [1024, 256], replicated, may hold values from -0.1875 to 0.1875
Outputs:
- result: bfloat16 [8192, 256], P(('groups', 'seq')), parts along dimension 0
There are 2 independent parts, one for each index of `groups`. A program takes and returns all parts, laid end to end along the dimension named above; an argument that names none is the same for every part. Nothing has to cross between parts.
All inputs are finite; a program needn't handle non-finite values.
Results may differ from a plain program's by a relative error of at most 0.013.
Values may be sent and summed in bfloat16 or wider, within the bound.
A program may use at most 64 MiB of HBM per device.

v0:
```python
import math

import jax
import jax.numpy as jnp
from jax import lax
from jax.sharding import PartitionSpec as P

exact = lax.Precision.HIGHEST
epsilon = 1e-06


def passed_along(value, axis, steps):
    count = lax.axis_size(axis)
    first, last = (max(0, -steps), min(count, count - steps))
    return lax.ppermute(value, axis, [(source, source + steps) for source in range(first, last)])


def as_sent(array):
    return jax.tree.map(lambda a: a.astype(jnp.bfloat16) if a.dtype == jnp.float32 else a, array)


def rms_scale(values, gain):
    wide = values.astype(jnp.float32)
    return wide * lax.rsqrt(jnp.mean(wide * wide, axis=-1, keepdims=True) + epsilon) * gain


def phase_table(out_start, out_count, in_start, in_count, period):
    index_out = out_start + lax.iota(jnp.int32, out_count)[:, None]
    index_in = in_start + lax.iota(jnp.int32, in_count)[None, :]
    angle = 2.0 * math.pi / period * (index_out * index_in % period).astype(jnp.float32)
    return (jnp.cos(angle), jnp.sin(angle))


def apply_filter(spec_real, spec_imag, filt):
    filt_real = filt[0].astype(jnp.float32)
    filt_imag = filt[1].astype(jnp.float32)
    return (
        spec_real * filt_real - spec_imag * filt_imag,
        spec_real * filt_imag + spec_imag * filt_real,
    )


def rows_forward_first(piece, column_start, total):
    half = piece.shape[0]
    length = 2 * half
    count = piece.shape[1]
    cosine, sine = phase_table(0, length, 0, half, length)
    wide = piece.astype(jnp.float32)
    real_part = jnp.einsum("kn,nmc->kmc", cosine, wide, precision=exact)
    imag_part = -jnp.einsum("kn,nmc->kmc", sine, wide, precision=exact)
    turn_cos, turn_sin = phase_table(0, length, column_start, count, total)
    turn_cos = turn_cos[:, :, None]
    turn_sin = turn_sin[:, :, None]
    return (
        real_part * turn_cos + imag_part * turn_sin,
        imag_part * turn_cos - real_part * turn_sin,
    )


def rows_forward_second(parts):
    real_part, imag_part = parts
    size = real_part.shape[1]
    cosine, sine = phase_table(0, size, 0, size, size)
    real_cos = jnp.einsum("kn,anc->akc", cosine, real_part, precision=exact)
    real_sin = jnp.einsum("kn,anc->akc", sine, real_part, precision=exact)
    imag_cos = jnp.einsum("kn,anc->akc", cosine, imag_part, precision=exact)
    imag_sin = jnp.einsum("kn,anc->akc", sine, imag_part, precision=exact)
    return (real_cos + imag_sin, imag_cos - real_sin)


def rows_inverse_second(real_part, imag_part, row_start, total):
    rows = real_part.shape[0]
    size = real_part.shape[1]
    cosine, sine = phase_table(0, size, 0, size, size)
    real_cos = jnp.einsum("nk,akc->anc", cosine, real_part, precision=exact)
    real_sin = jnp.einsum("nk,akc->anc", sine, real_part, precision=exact)
    imag_cos = jnp.einsum("nk,akc->anc", cosine, imag_part, precision=exact)
    imag_sin = jnp.einsum("nk,akc->anc", sine, imag_part, precision=exact)
    out_real = real_cos - imag_sin
    out_imag = real_sin + imag_cos
    turn_cos, turn_sin = phase_table(row_start, rows, 0, size, total)
    turn_cos = turn_cos[:, :, None]
    turn_sin = turn_sin[:, :, None]
    return (out_real * turn_cos - out_imag * turn_sin, out_real * turn_sin + out_imag * turn_cos)


def rows_inverse_first(parts, total):
    real_part, imag_part = parts
    length = real_part.shape[0]
    half = length // 2
    cosine, sine = phase_table(0, half, 0, length, length)
    summed = jnp.einsum("nk,kmc->nmc", cosine, real_part, precision=exact) - jnp.einsum(
        "nk,kmc->nmc", sine, imag_part, precision=exact
    )
    return summed / total


def local(
    tokens,
    norm_gain,
    in_weight,
    short_filter,
    spectra,
    skip_gain,
    out_weight,
    mlp_gain,
    up_weight,
    down_weight,
):
    tok_rows, width = tokens.shape
    devices = lax.axis_size("seq")
    position = lax.axis_index("seq")
    total = 2 * tok_rows * devices
    inner = min(tok_rows, 512)
    outer = total // inner
    normed = rms_scale(tokens, norm_gain).astype(jnp.bfloat16)
    projected = jnp.dot(normed, in_weight, preferred_element_type=jnp.float32).astype(jnp.bfloat16)
    taps = short_filter.shape[0]
    earlier = passed_along(projected[tok_rows - (taps - 1) :], "seq", 1)
    extended = jnp.concatenate([earlier, projected], axis=0).astype(jnp.float32)
    mixed = short_filter[0] * extended[taps - 1 :]
    for lag in range(1, taps):
        mixed = mixed + short_filter[lag] * extended[taps - 1 - lag : taps - 1 - lag + tok_rows]
    query = mixed[:, :width].astype(jnp.bfloat16)
    driven = (mixed[:, width : 2 * width] * mixed[:, 2 * width :]).astype(jnp.bfloat16)
    local_cols = inner // devices
    col_start = position * local_cols
    blocked = driven.reshape(tok_rows // inner, inner, width)
    piece = lax.all_to_all(blocked, "seq", split_axis=1, concat_axis=0, tiled=True)
    real_part, imag_part = rows_forward_first(piece, col_start, total)
    spec_real, spec_imag = rows_forward_second(
        (
            lax.all_to_all(
                real_part.astype(jnp.bfloat16), "seq", split_axis=0, concat_axis=1, tiled=True
            ).astype(real_part.dtype),
            lax.all_to_all(
                imag_part.astype(jnp.bfloat16), "seq", split_axis=0, concat_axis=1, tiled=True
            ).astype(imag_part.dtype),
        )
    )
    resident = jnp.transpose(spectra, (0, 2, 3, 1))
    prod_real, prod_imag = apply_filter(spec_real, spec_imag, resident)
    local_rows = outer // devices
    back_real, back_imag = rows_inverse_second(prod_real, prod_imag, position * local_rows, total)
    response_cols = rows_inverse_first(
        (
            lax.all_to_all(
                as_sent(back_real), "seq", split_axis=1, concat_axis=0, tiled=True
            ).astype(back_real.dtype),
            lax.all_to_all(
                as_sent(back_imag), "seq", split_axis=1, concat_axis=0, tiled=True
            ).astype(back_imag.dtype),
        ),
        total,
    )
    response_cols = response_cols + skip_gain[None, None, :] * piece.astype(jnp.float32)
    response = lax.all_to_all(
        response_cols, "seq", split_axis=0, concat_axis=1, tiled=True
    ).reshape(tok_rows, width)
    gated = (query.astype(jnp.float32) * response).astype(jnp.bfloat16)
    hidden_state = (
        tokens.astype(jnp.float32) + jnp.dot(gated, out_weight, preferred_element_type=jnp.float32)
    ).astype(jnp.bfloat16)
    second_norm = rms_scale(hidden_state, mlp_gain).astype(jnp.bfloat16)
    activated = jax.nn.gelu(
        jnp.dot(second_norm, up_weight, preferred_element_type=jnp.float32), approximate=True
    ).astype(jnp.bfloat16)
    return (
        hidden_state.astype(jnp.float32)
        + jnp.dot(activated, down_weight, preferred_element_type=jnp.float32)
    ).astype(jnp.bfloat16)


def solution(mesh):
    in_specs = (
        P(("groups", "seq"), None),
        P(),
        P(),
        P(),
        P(None, None, "seq", None),
        P(),
        P(),
        P(),
        P(),
        P(),
    )
    out_specs = P(("groups", "seq"), None)
    return jax.shard_map(local, mesh=mesh, in_specs=in_specs, out_specs=out_specs, check_vma=False)
```

profile of v0, /device:TPU:0, one launch (start us, length us, event | category | flops | bytes accessed | tf_op | source)
XLA Modules:
  0.0 113.2 jit_solution(16862313538930423906)
XLA Ops:
  0.0 1.1 copy.59
  2.2 2.4 %collective-permute-start = (bf16[2,768]{1,0:T(2,128)(2,1)S(1)}, bf16[2,768]{1,0:T(2,128)(2,1)S(1)}, u32[]{:S(2)}, u32[]{:S(2)}) collective-permute-start(bf16[2,768]{1,0:T(2,128)(2,1)S(1)} %slice.49), channel_id=1, source_target_pairs={{0,1},{1,2},{2,3},{3,4},{4,5},{5,6},{6,7},{7,8},{8,9},{9,10},{10,1... | collective-permute-start | bytes 9224 | tf_op jit(solution)/shard_map/ppermute | solution.py:15
  6.5 1.4 %reduce.6 = bf16[256,256]{1,0:T(8,128)(2,1)S(1)} reduce(bf16[256,1,256]{2,1,0:T(2,128)(2,1)S(1)} %bitcast.118, bf16[]{:T(256)} %broadcast.303), dimensions={1}, to_apply=%bitcast.110.reduce_sub_computation | reduce | bytes 262146
  8.6 9.1 %all-to-all-start = ((bf16[16,2,2048]{2,1,0:T(2,128)(2,1)}), bf16[16,2,2048]{2,1,0:T(2,128)(2,1)S(1)}, u32[]{:S(2)}, u32[]{:S(2)}) async-start(bf16[16,2,2048]{2,1,0:T(2,128)(2,1)} %reshape.163), calls=%async_computation | async-start | bytes 262144 | tf_op jit(solution)/shard_map/all_to_all | solution.py:129
  17.9 7.8 %all-to-all-done = bf16[16,2,2048]{2,1,0:T(2,128)(2,1)S(1)} async-done(((bf16[16,2,2048]{2,1,0:T(2,128)(2,1)}), bf16[16,2,2048]{2,1,0:T(2,128)(2,1)S(1)}, u32[]{:S(2)}, u32[]{:S(2)}) %all-to-all-start) | async-done | bytes 131104 | tf_op jit(solution)/shard_map/all_to_all | solution.py:129
  27.7 3.5 %all-to-all-start.1 = ((bf16[32,16,256]{2,1,0:T(8,128)(2,1)}), bf16[32,16,256]{2,1,0:T(8,128)(2,1)S(1)}, u32[]{:S(2)}, u32[]{:S(2)}) async-start(bf16[32,16,256]{2,1,0:T(8,128)(2,1)} %copy.63), calls=%async_computation.1 | async-start | bytes 524288 | tf_op jit(solution)/shard_map/all_to_all | solution.py:133
  32.1 9.2 %all-to-all-done.1 = bf16[32,16,256]{2,1,0:T(8,128)(2,1)S(1)} async-done(((bf16[32,16,256]{2,1,0:T(8,128)(2,1)}), bf16[32,16,256]{2,1,0:T(8,128)(2,1)S(1)}, u32[]{:S(2)}, u32[]{:S(2)}) %all-to-all-start.1) | async-done | bytes 262176 | tf_op jit(solution)/shard_map/all_to_all | solution.py:133
  41.3 3.7 %all-to-all-start.2 = ((bf16[32,16,256]{2,1,0:T(8,128)(2,1)}), bf16[32,16,256]{2,1,0:T(8,128)(2,1)S(1)}, u32[]{:S(2)}, u32[]{:S(2)}) async-start(bf16[32,16,256]{2,1,0:T(8,128)(2,1)} %copy.66), calls=%async_computation.2 | async-start | bytes 524288 | tf_op jit(solution)/shard_map/all_to_all | solution.py:136
  45.3 9.6 %all-to-all-done.2 = bf16[32,16,256]{2,1,0:T(8,128)(2,1)S(1)} async-done(((bf16[32,16,256]{2,1,0:T(8,128)(2,1)}), bf16[32,16,256]{2,1,0:T(8,128)(2,1)S(1)}, u32[]{:S(2)}, u32[]{:S(2)}) %all-to-all-start.2) | async-done | bytes 262176 | tf_op jit(solution)/shard_map/all_to_all | solution.py:136
  54.8 1.4 %fusion.42 = f32[2,256,256]{2,1,0:T(8,128)S(1)} fusion(bf16[2,256,256]{2,1,0:T(8,128)(2,1)S(1)} %bitcast.126), kind=kOutput, calls=%fused_computation.74 | convolution fusion | flops 403570688 | bytes 786432 | tf_op jit(solution)/shard_map/kn,anc->akc/dot_general | solution.py:66
  56.3 1.4 %fusion.44 = f32[2,256,256]{2,1,0:T(8,128)S(1)} fusion(bf16[2,256,256]{2,1,0:T(8,128)(2,1)S(1)} %bitcast.124), kind=kOutput, calls=%fused_computation.76 | convolution fusion | flops 403570688 | bytes 786432 | tf_op jit(solution)/shard_map/kn,anc->akc/dot_general | solution.py:64
  57.7 1.4 %fusion = f32[2,256,256]{1,2,0:T(8,128)S(1)} fusion(f32[2,256,256]{2,1,0:T(8,128)S(1)} %fusion.42, bf16[2,256,256]{2,1,0:T(8,128)(2,1)S(1)} %bitcast.125), kind=kOutput, calls=%fused_computation.4 | convolution fusion | flops 403701760 | bytes 1310720 | tf_op jit(solution)/shard_map/kn,anc->akc/dot_general | solution.py:65
  59.1 1.4 %fusion.1 = f32[2,256,256]{1,2,0:T(8,128)S(1)} fusion(f32[2,256,256]{2,1,0:T(8,128)S(1)} %fusion.44, bf16[2,256,256]{2,1,0:T(8,128)(2,1)S(1)} %bitcast.127), kind=kOutput, calls=%fused_computation.6 | convolution fusion | flops 403701760 | bytes 1310720 | tf_op jit(solution)/shard_map/kn,anc->akc/dot_general | solution.py:67
  60.5 1.6 %fusion.34 = f32[2,256,256]{2,1,0:T(8,128)S(1)} fusion(f32[2,256,256]{1,2,0:T(8,128)S(1)} %fusion, f32[2,256,256]{1,2,0:T(8,128)S(1)} %fusion.1, bf16[2,2,256,256]{2,3,1,0:T(8,128)(2,1)S(1)} %bitcast.114), kind=kOutput, calls=%fused_computation.66 | convolution fusion | flops 404226048 | bytes 2097152 | tf_op jit(solution)/shard_map/nk,akc->anc/dot_general | solution.py:76
  62.1 1.6 %fusion.40 = f32[2,256,256]{2,1,0:T(8,128)S(1)} fusion(f32[2,256,256]{1,2,0:T(8,128)S(1)} %fusion, f32[2,256,256]{1,2,0:T(8,128)S(1)} %fusion.1, bf16[2,2,256,256]{2,3,1,0:T(8,128)(2,1)S(1)} %bitcast.115), kind=kOutput, calls=%fused_computation.72 | convolution fusion | flops 404226048 | bytes 2097152 | tf_op jit(solution)/shard_map/nk,akc->anc/dot_general | solution.py:75
  63.8 1.6 %convolution_add_fusion.1 = f32[2,256,256]{2,1,0:T(8,128)S(1)} fusion(f32[2,256,256]{2,1,0:T(8,128)S(1)} %fusion.34, f32[2,256,256]{1,2,0:T(8,128)S(1)} %fusion.1, f32[2,256,256]{1,2,0:T(8,128)S(1)} %fusion, bf16[2,2,256,256]{2,3,1,0:T(8,128)(2,1)S(1)} %bitcast.116), kind=kOutput, calls=%fused_computation.7 | convolution fusion | flops 404357120 | bytes 2621440 | tf_op jit(solution)/shard_map/nk,akc->anc/dot_general | solution.py:77
  65.4 1.9 %fusion.31 = (bf16[2,256,256]{1,2,0:T(8,128)(2,1)S(1)}, bf16[2,256,256]{1,2,0:T(8,128)(2,1)S(1)}) fusion(f32[2,256,256]{2,1,0:T(8,128)S(1)} %convolution_add_fusion.1, f32[2,256]{1,0:T(2,128)S(1)} %get-tuple-element.13, f32[2,256]{1,0:T(2,128)S(1)} %get-tuple-element.12, f32[2,256,256]{2,1,0:T(8,128)S(1)} %fusion.40, f32[2,256,256]{1,2,0:T(8,128)S(1)} %fusion.1, ...), kind=kOutput, calls=%fused_computation.58 | convolution fusion | flops 405405696 | bytes 3149824 | tf_op jit(solution)/shard_map/nk,akc->anc/dot_general | solution.py:78
  67.3 0.9 copy.75
  68.1 3.5 %all-to-all-start.4 = ((bf16[2,256,256]{2,0,1:T(2,128)(2,1)}), bf16[2,256,256]{2,0,1:T(2,128)(2,1)S(1)}, u32[]{:S(2)}, u32[]{:S(2)}) async-start(bf16[2,256,256]{2,0,1:T(2,128)(2,1)} %copy.75), calls=%async_computation.4 | async-start | bytes 524288 | tf_op jit(solution)/shard_map/all_to_all | solution.py:150
  72.5 9.1 %all-to-all-done.4 = bf16[2,256,256]{2,0,1:T(2,128)(2,1)S(1)} async-done(((bf16[2,256,256]{2,0,1:T(2,128)(2,1)}), bf16[2,256,256]{2,0,1:T(2,128)(2,1)S(1)}, u32[]{:S(2)}, u32[]{:S(2)}) %all-to-all-start.4) | async-done | bytes 262176 | tf_op jit(solution)/shard_map/all_to_all | solution.py:150
  81.7 3.5 %all-to-all-start.3 = ((bf16[2,256,256]{2,0,1:T(2,128)(2,1)}), bf16[2,256,256]{2,0,1:T(2,128)(2,1)S(1)}, u32[]{:S(2)}, u32[]{:S(2)}) async-start(bf16[2,256,256]{2,0,1:T(2,128)(2,1)} %copy.72), calls=%async_computation.3 | async-start | bytes 524288 | tf_op jit(solution)/shard_map/all_to_all | solution.py:147
  85.7 9.6 %all-to-all-done.3 = bf16[2,256,256]{2,0,1:T(2,128)(2,1)S(1)} async-done(((bf16[2,256,256]{2,0,1:T(2,128)(2,1)}), bf16[2,256,256]{2,0,1:T(2,128)(2,1)S(1)}, u32[]{:S(2)}, u32[]{:S(2)}) %all-to-all-start.3) | async-done | bytes 262176 | tf_op jit(solution)/shard_map/all_to_all | solution.py:147
  96.8 12.8 %all_to_all.93 = f32[16,16,256]{2,1,0:T(8,128)S(1)} all-to-all(f32[16,16,256]{2,1,0:T(8,128)S(1)} %copy.79), channel_id=1, replica_groups=mesh['groups'=2,'seq'=16] {'seq'}, dimensions={0} | all-to-all | bytes 524288 | tf_op jit(solution)/shard_map/all_to_all | solution.py:157
  111.5 0.9 fusion.6
  (57 shorter events, 12.3 us)
Async XLA Ops:
  0.0 110.8 %copy-start = (bf16[1024,256]{1,0:T(8,128)(2,1)S(1)}, bf16[1024,256]{1,0:T(8,128)(2,1)}, u32[]{:S(2)}) copy-start(bf16[1024,256]{1,0:T(8,128)(2,1)} %param.19) | copy-start | bytes 1572868
  0.0 1.2 %copy-start.2 = (bf16[256,768]{1,0:T(8,128)(2,1)S(1)}, bf16[256,768]{1,0:T(8,128)(2,1)}, u32[]{:S(2)}) copy-start(bf16[256,768]{1,0:T(8,128)(2,1)} %param.12) | copy-start | bytes 1179652
  1.1 0.7 copy-start.5
  1.8 2.8 %copy-start.4 = (f32[3,768]{1,0:T(4,128)S(1)}, f32[3,768]{1,0:T(4,128)}, u32[]{:S(2)}) copy-start(f32[3,768]{1,0:T(4,128)} %param.13) | copy-start | bytes 27652
  2.2 3.2 %collective-permute-start = (bf16[2,768]{1,0:T(2,128)(2,1)S(1)}, bf16[2,768]{1,0:T(2,128)(2,1)S(1)}, u32[]{:S(2)}, u32[]{:S(2)}) collective-permute-start(bf16[2,768]{1,0:T(2,128)(2,1)S(1)} %slice.49), channel_id=1, source_target_pairs={{0,1},{1,2},{2,3},{3,4},{4,5},{5,6},{6,7},{7,8},{8,9},{9,10},{10,1... | collective-permute-start | bytes 9224 | tf_op jit(solution)/shard_map/ppermute | solution.py:15
  8.6 17.0 %all-to-all-start = ((bf16[16,2,2048]{2,1,0:T(2,128)(2,1)}), bf16[16,2,2048]{2,1,0:T(2,128)(2,1)S(1)}, u32[]{:S(2)}, u32[]{:S(2)}) async-start(bf16[16,2,2048]{2,1,0:T(2,128)(2,1)} %reshape.163), calls=%async_computation | async-start | bytes 262144 | tf_op jit(solution)/shard_map/all_to_all | solution.py:129
  27.7 13.5 %all-to-all-start.1 = ((bf16[32,16,256]{2,1,0:T(8,128)(2,1)}), bf16[32,16,256]{2,1,0:T(8,128)(2,1)S(1)}, u32[]{:S(2)}, u32[]{:S(2)}) async-start(bf16[32,16,256]{2,1,0:T(8,128)(2,1)} %copy.63), calls=%async_computation.1 | async-start | bytes 524288 | tf_op jit(solution)/shard_map/all_to_all | solution.py:133
  31.3 13.7 %copy-start.1 = (bf16[2,256,2,256]{3,2,1,0:T(2,128)(2,1)S(1)}, bf16[2,256,2,256]{3,2,1,0:T(2,128)(2,1)}, u32[]{:S(2)}) copy-start(bf16[2,256,2,256]{3,2,1,0:T(2,128)(2,1)} %param.14) | copy-start | bytes 1572868
  41.3 13.5 %all-to-all-start.2 = ((bf16[32,16,256]{2,1,0:T(8,128)(2,1)}), bf16[32,16,256]{2,1,0:T(8,128)(2,1)S(1)}, u32[]{:S(2)}, u32[]{:S(2)}) async-start(bf16[32,16,256]{2,1,0:T(8,128)(2,1)} %copy.66), calls=%async_computation.2 | async-start | bytes 524288 | tf_op jit(solution)/shard_map/all_to_all | solution.py:136
  68.1 13.5 %all-to-all-start.4 = ((bf16[2,256,256]{2,0,1:T(2,128)(2,1)}), bf16[2,256,256]{2,0,1:T(2,128)(2,1)S(1)}, u32[]{:S(2)}, u32[]{:S(2)}) async-start(bf16[2,256,256]{2,0,1:T(2,128)(2,1)} %copy.75), calls=%async_computation.4 | async-start | bytes 524288 | tf_op jit(solution)/shard_map/all_to_all | solution.py:150
  81.7 13.5 %all-to-all-start.3 = ((bf16[2,256,256]{2,0,1:T(2,128)(2,1)}), bf16[2,256,256]{2,0,1:T(2,128)(2,1)S(1)}, u32[]{:S(2)}, u32[]{:S(2)}) async-start(bf16[2,256,256]{2,0,1:T(2,128)(2,1)} %copy.72), calls=%async_computation.3 | async-start | bytes 524288 | tf_op jit(solution)/shard_map/all_to_all | solution.py:147
  95.7 0.7 copy-start.6
  109.6 0.9 copy-start.3
  109.7 1.2 %copy-start.7 = (bf16[256,1024]{1,0:T(8,128)(2,1)S(1)}, bf16[256,1024]{1,0:T(8,128)(2,1)}, u32[]{:S(2)}) copy-start(bf16[256,1024]{1,0:T(8,128)(2,1)} %param.18) | copy-start | bytes 1572868
  110.8 0.7 copy-start.8
where the time goes:
time: 114 us; the launch traced here: 113 us
  waiting for transfers between devices  46 us (40%)
  starting transfers between devices  25.8 us (23%)
  matrix products  15.6 us (14%)
  blocking collectives  12.8 us (11%)
  local copies, waits for them, and re-layouts  10.5 us (9%)
  other arithmetic  2.12 us (2%)
    all_to_all x1, blocking collectives, local(): lax.all_to_all(response_cols, 'seq', split_axis=0, concat_axis=1, tiled=T...  12.8 us
    all_to_all x1, waiting for transfers between devices, local(): lax.all_to_all(as_sent(back_real), 'seq', split_axis=1, concat_axis=0, ti...  9.58 us
    all_to_all x1, waiting for transfers between devices, local(): lax.all_to_all(imag_part.astype(jnp.bfloat16), 'seq', split_axis=0, conca...  9.56 us
    all_to_all x1, waiting for transfers between devices, local(): lax.all_to_all(real_part.astype(jnp.bfloat16), 'seq', split_axis=0, conca...  9.15 us
    all_to_all x1, waiting for transfers between devices, local(): lax.all_to_all(as_sent(back_imag), 'seq', split_axis=1, concat_axis=0, ti...  9.15 us
    all_to_all x1, starting transfers between devices, local(): lax.all_to_all(blocked, 'seq', split_axis=1, concat_axis=0, tiled=True)  9.1 us
    all_to_all x1, waiting for transfers between devices, local(): lax.all_to_all(blocked, 'seq', split_axis=1, concat_axis=0, tiled=True)  7.79 us
    unnamed x24, local copies, waits for them, and re-layouts  5.05 us
  transfers between devices with their start and end apart: 6, of which 6 were waited for; matrix products, arithmetic and copies ran while one was open for 2% of the time, Pallas kernels for 0%

commit v1 on v0

--- a/solution.py
+++ b/solution.py
@@ -1,8 +1,13 @@
+import functools
 import math
 
 import jax
 import jax.numpy as jnp
+import ml_dtypes
+import numpy as np
 from jax import lax
+from jax.experimental import pallas as pl
+from jax.experimental.pallas import tpu as pltpu
 from jax.sharding import PartitionSpec as P
 
 exact = lax.Precision.HIGHEST
@@ -171,6 +176,261 @@
     ).astype(jnp.bfloat16)
 
 
+MESH = pl.DeviceIdType.MESH
+
+
+def dft_tables(n, outer, inner, groups, share):
+    kl = outer // n
+    k1 = np.arange(outer)
+    ang = 2.0 * np.pi * (np.outer(k1, np.arange(n)) % outer) / outer
+    weights = np.stack([np.cos(ang), -np.sin(ang)]).reshape(2, n, kl, n)
+    first = np.einsum("rpkn,gh,ij->rgpiknhj", weights, np.eye(groups), np.eye(share))
+    first = first.reshape(2 * groups * outer * share, n * groups * share)
+    ang = 2.0 * np.pi * (np.outer(np.arange(inner), np.arange(inner)) % inner) / inner
+    cos, sin = np.cos(ang), np.sin(ang)
+    second = np.block([[cos, -sin], [sin, cos]])
+    ang = 2.0 * np.pi * np.outer(k1, np.arange(inner)) / (outer * inner)
+    turn = np.stack([np.cos(ang), np.sin(ang)]).reshape(2, n, 1, kl, inner)
+    turn = np.broadcast_to(turn, (2, n, share, kl, inner)).reshape(2, n * share * kl, inner)
+    low = lambda a: a.astype(ml_dtypes.bfloat16)
+    return low(first), low(np.ascontiguousarray(first.T)), low(second), turn.astype(np.float32)
+
+
+def kernel(
+    groups, n, share,
+    tokens, norm_gain, in_weight, short_filter, skip_gain, mlp_gain,
+    spectra, out_hbm, up_hbm, down_hbm, first_hbm, last_hbm, second_hbm, turn_hbm,
+    result,
+    filt, halo, extended, sent, signal, back, response,
+    out_weight, up_weight, down_weight, first, last, second, turn,
+    local_sem, filt_send, filt_recv, halo_send, halo_recv,
+    sig_send, sig_recv, resp_send, resp_recv,
+):
+    count = groups * n
+    group = lax.axis_index("groups")
+    position = lax.axis_index("seq")
+    me = position * groups + group
+    rows, width = tokens.shape
+    taps = short_filter.shape[0]
+
+    def place(index):
+        return (lax.rem(index, groups), lax.div(index, groups))
+
+    barrier = pltpu.get_barrier_semaphore()
+
+    def greet(step, carry):
+        pl.semaphore_signal(
+            barrier, inc=1, device_id=place(lax.rem(me + step, count)), device_id_type=MESH
+        )
+        return carry
+
+    lax.fori_loop(1, count, greet, 0)
+
+    pairs = (
+        (first_hbm, first), (second_hbm, second), (turn_hbm, turn), (last_hbm, last),
+        (out_hbm, out_weight), (up_hbm, up_weight), (down_hbm, down_weight),
+    )
+    loads = [
+        pltpu.make_async_copy(source, target, local_sem.at[i])
+        for i, (source, target) in enumerate(pairs)
+    ]
+
+    def channels(seq_index):
+        return pl.ds((seq_index * groups + group) * share, share)
+
+    own_filter = pltpu.make_async_copy(
+        spectra.at[:, channels(position)], filt.at[position], local_sem.at[len(pairs)]
+    )
+
+    def filter_copy(target, source):
+        return pltpu.make_async_remote_copy(
+            src_ref=spectra.at[:, channels(target)], dst_ref=filt.at[source],
+            send_sem=filt_send.at[target], recv_sem=filt_recv.at[source],
+            device_id=(group, target), device_id_type=MESH,
+        )
+
+    def halo_copy(target):
+        return pltpu.make_async_remote_copy(
+            src_ref=tokens.at[pl.ds(rows - 16, 16)], dst_ref=halo,
+            send_sem=halo_send.at[0], recv_sem=halo_recv.at[0],
+            device_id=(group, target), device_id_type=MESH,
+        )
+
+    def signal_copy(target, source):
+        return pltpu.make_async_remote_copy(
+            src_ref=sent.at[target], dst_ref=signal.at[source],
+            send_sem=sig_send.at[target], recv_sem=sig_recv.at[source],
+            device_id=place(target), device_id_type=MESH,
+        )
+
+    def response_copy(target, source):
+        return pltpu.make_async_remote_copy(
+            src_ref=back.at[target], dst_ref=response.at[source],
+            send_sem=resp_send.at[target], recv_sem=resp_recv.at[source],
+            device_id=place(target), device_id_type=MESH,
+        )
+
+    def each(total, own, action):
+        def body(step, carry):
+            action(lax.rem(own + step, total))
+            return carry
+
+        lax.fori_loop(1, total, body, 0)
+
+    for load in loads:
+        load.start()
+    own_filter.start()
+    pl.semaphore_wait(barrier, count - 1)
+
+    @pl.when(position < n - 1)
+    def _():
+        halo_copy(position + 1).start()
+
+    @pl.when(position == 0)
+    def _():
+        halo[...] = jnp.zeros_like(halo)
+
+    each(n, position, lambda other: filter_copy(other, position).start())
+
+    gain = norm_gain[...].reshape(1, width)
+    weight = in_weight[...]
+
+    def project(values):
+        normed = rms_scale(values, gain).astype(jnp.bfloat16)
+        made = jnp.dot(normed, weight, preferred_element_type=jnp.float32)
+        return made.astype(jnp.bfloat16).astype(jnp.float32)
+
+    extended[pl.ds(8, rows), :] = project(tokens[...])
+
+    @pl.when(position > 0)
+    def _():
+        halo_copy(position).wait_recv()
+
+    extended[pl.ds(0, 8), :] = project(halo[...])[8:, :]
+    mixed = short_filter[0:1, :] * extended[pl.ds(8, rows), :]
+    for lag in range(1, taps):
+        mixed = mixed + short_filter[lag : lag + 1, :] * extended[pl.ds(8 - lag, rows), :]
+    query = mixed[:, :width].astype(jnp.bfloat16).astype(jnp.float32)
+    driven = (mixed[:, width : 2 * width] * mixed[:, 2 * width :]).astype(jnp.bfloat16)
+    driven = driven.astype(jnp.float32)
+    sent[...] = driven.T.reshape(count, share, rows).astype(jnp.bfloat16)
+    each(count, me, lambda other: signal_copy(other, me).start())
+    signal[pl.ds(me, 1)] = sent[pl.ds(me, 1)]
+
+    for load in loads:
+        load.wait()
+    own_filter.wait()
+    each(count, me, lambda other: signal_copy(me, other).wait_recv())
+
+    half = groups * n * share * (filt.shape[3])
+    bins = half // groups
+    gathered = signal[...].astype(jnp.float32).reshape(count * share, rows).astype(jnp.bfloat16)
+    part = jnp.dot(first[...], gathered, preferred_element_type=jnp.float32)
+    part_real = part[:half].reshape(groups, bins, rows)
+    part_imag = part[half:].reshape(groups, bins, rows)
+    turn_cos, turn_sin = turn[0][None], turn[1][None]
+    turned = jnp.concatenate(
+        [part_real * turn_cos + part_imag * turn_sin, part_imag * turn_cos - part_real * turn_sin],
+        axis=-1,
+    ).reshape(half, 2 * rows).astype(jnp.bfloat16)
+    spec = jnp.dot(turned, second[...], preferred_element_type=jnp.float32)
+    spec_real = spec[:, :rows].reshape(groups, bins, rows)
+    spec_imag = spec[:, rows:].reshape(groups, bins, rows)
+    each(n, position, lambda other: filter_copy(position, other).wait_recv())
+    filt_real = filt[:, 0].astype(jnp.float32).reshape(1, bins, rows)
+    filt_imag = filt[:, 1].astype(jnp.float32).reshape(1, bins, rows)
+    product = jnp.concatenate(
+        [
+            spec_real * filt_real - spec_imag * filt_imag,
+            -(spec_real * filt_imag + spec_imag * filt_real),
+        ],
+        axis=-1,
+    ).reshape(half, 2 * rows).astype(jnp.bfloat16)
+    inner_back = jnp.dot(product, second[...], preferred_element_type=jnp.float32)
+    back_real = inner_back[:, :rows].reshape(groups, bins, rows)
+    back_imag = inner_back[:, rows:].reshape(groups, bins, rows)
+    turned_back = jnp.concatenate(
+        [
+            (back_real * turn_cos + back_imag * turn_sin).reshape(half, rows),
+            (back_real * turn_sin - back_imag * turn_cos).reshape(half, rows),
+        ],
+        axis=0,
+    ).astype(jnp.bfloat16)
+    total = 2 * n * rows
+    conv = jnp.dot(last[...], turned_back, preferred_element_type=jnp.float32) * (1.0 / total)
+    back[...] = conv.reshape(count, share, rows).astype(jnp.bfloat16)
+    each(count, me, lambda other: response_copy(other, me).start())
+    response[pl.ds(me, 1)] = back[pl.ds(me, 1)]
+    each(count, me, lambda other: response_copy(me, other).wait_recv())
+
+    answer = response[...].astype(jnp.float32).reshape(width, rows).T
+    answer = answer + skip_gain[...].reshape(1, width) * driven
+    gated = (query * answer).astype(jnp.bfloat16)
+    hidden = (
+        tokens[...].astype(jnp.float32)
+        + jnp.dot(gated, out_weight[...], preferred_element_type=jnp.float32)
+    ).astype(jnp.bfloat16)
+    second_norm = rms_scale(hidden, mlp_gain[...].reshape(1, width)).astype(jnp.bfloat16)
+    activated = jax.nn.gelu(
+        jnp.dot(second_norm, up_weight[...], preferred_element_type=jnp.float32), approximate=True
+    ).astype(jnp.bfloat16)
+    result[...] = (
+        hidden.astype(jnp.float32)
+        + jnp.dot(activated, down_weight[...], preferred_element_type=jnp.float32)
+    ).astype(jnp.bfloat16)
+
+    @pl.when(position < n - 1)
+    def _():
+        halo_copy(position + 1).wait_send()
+
+    each(n, position, lambda other: filter_copy(other, position).wait_send())
+    each(count, me, lambda other: signal_copy(other, me).wait_send())
+    each(count, me, lambda other: response_copy(other, me).wait_send())
+
+
+def fused(
+    tokens, norm_gain, in_weight, short_filter, spectra, skip_gain,
+    out_weight, mlp_gain, up_weight, down_weight,
+):
+    rows, width = tokens.shape
+    groups, n = lax.axis_size("groups"), lax.axis_size("seq")
+    count = groups * n
+    share = width // count
+    local_outer = spectra.shape[2]
+    first, last, second, turn = dft_tables(n, n * local_outer, rows, groups, share)
+    low = jnp.bfloat16
+    vmem = pl.BlockSpec(memory_space=pltpu.VMEM)
+    far = pl.BlockSpec(memory_space=pl.ANY)
+    dma = pltpu.SemaphoreType.DMA
+    held = [out_weight, up_weight, down_weight, first, last, second, turn]
+    return pl.pallas_call(
+        functools.partial(kernel, groups, n, share),
+        out_shape=jax.ShapeDtypeStruct((rows, width), low),
+        in_specs=[vmem] * 6 + [far] * 8,
+        out_specs=vmem,
+        scratch_shapes=[
+            pltpu.VMEM((n, 2, share, local_outer, rows), low),
+            pltpu.VMEM((16, width), low),
+            pltpu.VMEM((rows + 8, 3 * width), jnp.float32),
+            pltpu.VMEM((count, share, rows), low),
+            pltpu.VMEM((count, share, rows), low),
+            pltpu.VMEM((count, share, rows), low),
+            pltpu.VMEM((count, share, rows), low),
+        ]
+        + [pltpu.VMEM(a.shape, a.dtype) for a in held]
+        + [
+            dma((8,)), dma((n,)), dma((n,)), dma((1,)), dma((1,)),
+            dma((count,)), dma((count,)), dma((count,)), dma((count,)),
+        ],
+        compiler_params=pltpu.CompilerParams(
+            collective_id=0, has_side_effects=True, vmem_limit_bytes=40 * 1024 * 1024
+        ),
+    )(
+        tokens, norm_gain, in_weight, short_filter, skip_gain, mlp_gain,
+        spectra, out_weight, up_weight, down_weight, first, last, second, turn,
+    )
+
+
 def solution(mesh):
     in_specs = (
         P(("groups", "seq"), None),
@@ -185,4 +445,16 @@
         P(),
     )
     out_specs = P(("groups", "seq"), None)
-    return jax.shard_map(local, mesh=mesh, in_specs=in_specs, out_specs=out_specs, check_vma=False)
+
+    def layer(*args):
+        rows, width = args[0].shape
+        spectra = args[4]
+        fits = (
+            width % (8 * mesh.size) == 0
+            and rows == spectra.shape[3]
+            and spectra.shape[2] == 2
+            and rows % 128 == 0
+        )
+        return (fused if fits else local)(*args)
+
+    return jax.shard_map(layer, mesh=mesh, in_specs=in_specs, out_specs=out_specs, check_vma=False)

time: 114 us -> 42 us (0.37)
  waiting for transfers between devices: 46 us -> 0 us
  Pallas kernels: 0 us -> 27.9 us
  starting transfers between devices: 25.8 us -> 0 us
  matrix products: 15.6 us -> 0 us
  blocking collectives: 12.8 us -> 0 us
  local copies, waits for them, and re-layouts: 10.5 us -> 13.5 us
  other arithmetic: 2.12 us -> 0 us
    all_to_all x5 -> x0, waiting for transfers between devices: 45.2 us -> none  [the longest x1 9.58 us: local(): lax.all_to_all(as_sent(back_real), 'seq', split_axis=1, concat_axis=0, ti...]
    pallas_call x0 -> x1, Pallas kernels: none -> 27.9 us  [fused(): pl.pallas_call(functools.partial(kernel, groups, n, share), out_shape=jax...]
    all_to_all x5 -> x0, starting transfers between devices: 23.4 us -> none  [the longest x1 9.1 us: local(): lax.all_to_all(blocked, 'seq', split_axis=1, concat_axis=0, tiled=True)]
    dot_general x15 -> x0, matrix products: 15.6 us -> none  [the longest x1 1.9 us: rows_inverse_second(): imag_sin = jnp.einsum('nk,akc->anc', sine, imag_part, precision=exact)]
    all_to_all x1 -> x0, blocking collectives: 12.8 us -> none  [local(): lax.all_to_all(response_cols, 'seq', split_axis=0, concat_axis=1, tiled=T...]
    unnamed x24 -> x29, local copies, waits for them, and re-layouts: 5.05 us -> 13.5 us
    convert_element_type x5 -> x0, local copies, waits for them, and re-layouts: 4.2 us -> none  [the longest x2 1.74 us: as_sent(): a.astype(jnp.bfloat16)]
    ppermute x1 -> x0, starting transfers between devices: 2.36 us -> none  [passed_along(): lax.ppermute(value, axis, [(source, source + steps) for source in range(f...]
  transfers between devices with their start and end apart: 6 -> 0, of which waited for: 6 -> 0; matrix products, arithmetic and copies ran while one was open for 2% -> 0% of each run, Pallas kernels for 0% -> 0%
where the time goes in v1:
time: 42 us; the launch traced here: 41.4 us
  Pallas kernels  27.9 us (66%)
  local copies, waits for them, and re-layouts  13.5 us (32%)
    pallas_call x1, Pallas kernels, fused(): pl.pallas_call(functools.partial(kernel, groups, n, share), out_shape=jax...  27.9 us
    unnamed x29, local copies, waits for them, and re-layouts  13.5 us

profile of v1, /device:TPU:0, one launch (start us, length us, event | category | flops | bytes accessed | tf_op | source)
XLA Modules:
  0.0 41.4 jit_solution(7598536517160528242)
XLA Ops:
  0.0 0.0 copy-start
  0.0 1.0 %copy-done = bf16[2,256,2,256]{3,2,1,0:T(2,128)(2,1)S(1)} copy-done((bf16[2,256,2,256]{3,2,1,0:T(2,128)(2,1)S(1)}, bf16[2,256,2,256]{3,2,1,0:T(2,128)(2,1)}, u32[]{:S(2)}) %copy-start) | copy-done | bytes 524312
  1.0 0.0 copy-start.1
  1.0 1.0 %copy-done.1 = bf16[256,1024]{1,0:T(8,128)(2,1)S(1)} copy-done((bf16[256,1024]{1,0:T(8,128)(2,1)S(1)}, bf16[256,1024]{1,0:T(8,128)(2,1)}, u32[]{:S(2)}) %copy-start.1) | copy-done | bytes 524312
  2.1 0.0 copy-start.2
  2.1 1.0 %copy-done.2 = bf16[1024,256]{1,0:T(8,128)(2,1)S(1)} copy-done((bf16[1024,256]{1,0:T(8,128)(2,1)S(1)}, bf16[1024,256]{1,0:T(8,128)(2,1)}, u32[]{:S(2)}) %copy-start.2) | copy-done | bytes 524312
  3.1 0.0 copy-start.3
  3.1 1.0 %copy-done.3 = f32[2,256,256]{2,1,0:T(8,128)S(1)} copy-done((f32[2,256,256]{2,1,0:T(8,128)S(1)}, f32[2,256,256]{2,1,0:T(8,128)}, u32[]{:S(2)}) %copy-start.3) | copy-done | bytes 524312
  4.2 0.0 copy-start.4
  4.2 1.0 %copy-done.4 = bf16[512,512]{1,0:T(8,128)(2,1)S(1)} copy-done((bf16[512,512]{1,0:T(8,128)(2,1)S(1)}, bf16[512,512]{1,0:T(8,128)(2,1)}, u32[]{:S(2)}) %copy-start.4) | copy-done | bytes 524312
  5.2 1.0 %copy-done.5 = bf16[256,1024]{1,0:T(8,128)(2,1)S(1)} copy-done((bf16[256,1024]{1,0:T(8,128)(2,1)S(1)}, bf16[256,1024]{1,0:T(8,128)(2,1)}, u32[]{:S(2)}) %copy-start.5) | copy-done | bytes 524312
  6.3 0.0 copy-start.6
  6.3 1.0 %copy-done.6 = bf16[1024,256]{1,0:T(8,128)(2,1)S(1)} copy-done((bf16[1024,256]{1,0:T(8,128)(2,1)S(1)}, bf16[1024,256]{1,0:T(8,128)(2,1)}, u32[]{:S(2)}) %copy-start.6) | copy-done | bytes 524312
  7.3 0.0 copy-start.7
  7.3 1.0 %copy-done.7 = bf16[256,768]{1,0:T(8,128)(2,1)S(1)} copy-done((bf16[256,768]{1,0:T(8,128)(2,1)S(1)}, bf16[256,768]{1,0:T(8,128)(2,1)}, u32[]{:S(2)}) %copy-start.7) | copy-done | bytes 393240
  8.3 0.0 copy-start.8
  8.3 0.9 %copy-done.8 = bf16[256,256]{1,0:T(8,128)(2,1)S(1)} copy-done((bf16[256,256]{1,0:T(8,128)(2,1)S(1)}, bf16[256,256]{1,0:T(8,128)(2,1)}, u32[]{:S(2)}) %copy-start.8) | copy-done | bytes 131096
  9.2 0.9 %copy-done.9 = bf16[256,256]{1,0:T(8,128)(2,1)S(1)} copy-done((bf16[256,256]{1,0:T(8,128)(2,1)S(1)}, bf16[256,256]{1,0:T(8,128)(2,1)}, u32[]{:S(2)}) %copy-start.9) | copy-done | bytes 131096
  10.1 0.7 %copy-done.10 = f32[3,768]{1,0:T(4,128)S(1)} copy-done((f32[3,768]{1,0:T(4,128)S(1)}, f32[3,768]{1,0:T(4,128)}, u32[]{:S(2)}) %copy-start.10) | copy-done | bytes 9240
  10.8 0.7 %copy-done.11 = f32[256]{0:T(256)S(1)} copy-done((f32[256]{0:T(256)S(1)}, f32[256]{0:T(256)}, u32[]{:S(2)}) %copy-start.11) | copy-done | bytes 1048
  11.5 0.7 %copy-done.12 = f32[256]{0:T(256)S(1)} copy-done((f32[256]{0:T(256)S(1)}, f32[256]{0:T(256)}, u32[]{:S(2)}) %copy-start.12) | copy-done | bytes 1048
  12.2 0.7 %copy-done.13 = f32[256]{0:T(256)S(1)} copy-done((f32[256]{0:T(256)S(1)}, f32[256]{0:T(256)}, u32[]{:S(2)}) %copy-start.13) | copy-done | bytes 1048
  12.8 27.9 %shard_map.136 = bf16[256,256]{1,0:T(8,128)(2,1)S(1)} custom-call(bf16[256,256]{1,0:T(8,128)(2,1)S(1)} %copy-done.8, f32[256]{0:T(256)S(1)} %copy-done.11, bf16[256,768]{1,0:T(8,128)(2,1)S(1)} %copy-done.7, f32[3,768]{1,0:T(4,128)S(1)} %copy-done.10, f32[256]{0:T(256)S(1)} %copy-done.12, f32[256]{0:T(256)S(1)} %copy-done.13, ...), custom_call_target="tpu_custom_call" | custom-call | tf_op jit(solution)/shard_map/pallas_call | solution.py:406
  40.7 0.7 %copy.16 = bf16[256,256]{1,0:T(8,128)(2,1)} copy(bf16[256,256]{1,0:T(8,128)(2,1)S(1)} %shard_map.136) | data formatting | bytes 262144
  (6 shorter events, 0.0 us)
Async XLA Ops:
  0.0 1.0 %copy-start = (bf16[2,256,2,256]{3,2,1,0:T(2,128)(2,1)S(1)}, bf16[2,256,2,256]{3,2,1,0:T(2,128)(2,1)}, u32[]{:S(2)}) copy-start(bf16[2,256,2,256]{3,2,1,0:T(2,128)(2,1)} %spectra.1) | copy-start | bytes 1572868
  1.0 1.0 %copy-start.1 = (bf16[256,1024]{1,0:T(8,128)(2,1)S(1)}, bf16[256,1024]{1,0:T(8,128)(2,1)}, u32[]{:S(2)}) copy-start(bf16[256,1024]{1,0:T(8,128)(2,1)} %up_hbm.1) | copy-start | bytes 1572868
  2.1 1.0 %copy-start.2 = (bf16[1024,256]{1,0:T(8,128)(2,1)S(1)}, bf16[1024,256]{1,0:T(8,128)(2,1)}, u32[]{:S(2)}) copy-start(bf16[1024,256]{1,0:T(8,128)(2,1)} %down_hbm.1) | copy-start | bytes 1572868
  3.1 1.0 %copy-start.3 = (f32[2,256,256]{2,1,0:T(8,128)S(1)}, f32[2,256,256]{2,1,0:T(8,128)}, u32[]{:S(2)}) copy-start(f32[2,256,256]{2,1,0:T(8,128)} %constant.11.clone.turn_hbm) | copy-start | bytes 1572868
  4.2 1.0 %copy-start.4 = (bf16[512,512]{1,0:T(8,128)(2,1)S(1)}, bf16[512,512]{1,0:T(8,128)(2,1)}, u32[]{:S(2)}) copy-start(bf16[512,512]{1,0:T(8,128)(2,1)} %constant.10.clone.second_hbm) | copy-start | bytes 1572868
  5.2 1.0 %copy-start.5 = (bf16[256,1024]{1,0:T(8,128)(2,1)S(1)}, bf16[256,1024]{1,0:T(8,128)(2,1)}, u32[]{:S(2)}) copy-start(bf16[256,1024]{1,0:T(8,128)(2,1)} %constant.9.clone.last_hbm) | copy-start | bytes 1572868
  6.3 1.0 %copy-start.6 = (bf16[1024,256]{1,0:T(8,128)(2,1)S(1)}, bf16[1024,256]{1,0:T(8,128)(2,1)}, u32[]{:S(2)}) copy-start(bf16[1024,256]{1,0:T(8,128)(2,1)} %constant.8.clone.first_hbm) | copy-start | bytes 1572868
  7.3 1.0 %copy-start.7 = (bf16[256,768]{1,0:T(8,128)(2,1)S(1)}, bf16[256,768]{1,0:T(8,128)(2,1)}, u32[]{:S(2)}) copy-start(bf16[256,768]{1,0:T(8,128)(2,1)} %in_weight.1) | copy-start | bytes 1179652
  8.3 0.9 %copy-start.8 = (bf16[256,256]{1,0:T(8,128)(2,1)S(1)}, bf16[256,256]{1,0:T(8,128)(2,1)}, u32[]{:S(2)}) copy-start(bf16[256,256]{1,0:T(8,128)(2,1)} %tokens.1) | copy-start | bytes 393220
  9.2 0.9 %copy-start.9 = (bf16[256,256]{1,0:T(8,128)(2,1)S(1)}, bf16[256,256]{1,0:T(8,128)(2,1)}, u32[]{:S(2)}) copy-start(bf16[256,256]{1,0:T(8,128)(2,1)} %out_hbm.1) | copy-start | bytes 393220
  10.1 0.7 %copy-start.10 = (f32[3,768]{1,0:T(4,128)S(1)}, f32[3,768]{1,0:T(4,128)}, u32[]{:S(2)}) copy-start(f32[3,768]{1,0:T(4,128)} %short_filter.1) | copy-start | bytes 27652
  10.8 0.7 %copy-start.11 = (f32[256]{0:T(256)S(1)}, f32[256]{0:T(256)}, u32[]{:S(2)}) copy-start(f32[256]{0:T(256)} %norm_gain.1) | copy-start | bytes 3076
  11.5 0.7 %copy-start.12 = (f32[256]{0:T(256)S(1)}, f32[256]{0:T(256)}, u32[]{:S(2)}) copy-start(f32[256]{0:T(256)} %skip_gain.1) | copy-start | bytes 3076
  12.2 0.7 %copy-start.13 = (f32[256]{0:T(256)S(1)}, f32[256]{0:T(256)}, u32[]{:S(2)}) copy-start(f32[256]{0:T(256)} %mlp_gain.1) | copy-start | bytes 3076

commit v2 on v1

--- a/solution.py
+++ b/solution.py
@@ -198,9 +198,10 @@
 
 def kernel(
     groups, n, share,
-    tokens, norm_gain, in_weight, short_filter, skip_gain, mlp_gain,
+    tokens_hbm, norm_hbm, in_hbm, short_hbm, skip_hbm, mlp_hbm,
     spectra, out_hbm, up_hbm, down_hbm, first_hbm, last_hbm, second_hbm, turn_hbm,
     result,
+    tokens, norm_gain, in_weight, short_filter, skip_gain, mlp_gain,
     filt, halo, extended, sent, signal, back, response,
     out_weight, up_weight, down_weight, first, last, second, turn,
     local_sem, filt_send, filt_recv, halo_send, halo_recv,
@@ -226,9 +227,14 @@
 
     lax.fori_loop(1, count, greet, 0)
 
-    pairs = (
+    early = (
+        (tokens_hbm, tokens), (norm_hbm, norm_gain), (in_hbm, in_weight),
+        (short_hbm, short_filter),
+    )
+    pairs = early + (
         (first_hbm, first), (second_hbm, second), (turn_hbm, turn), (last_hbm, last),
         (out_hbm, out_weight), (up_hbm, up_weight), (down_hbm, down_weight),
+        (skip_hbm, skip_gain), (mlp_hbm, mlp_gain),
     )
     loads = [
         pltpu.make_async_copy(source, target, local_sem.at[i])
@@ -251,7 +257,7 @@
 
     def halo_copy(target):
         return pltpu.make_async_remote_copy(
-            src_ref=tokens.at[pl.ds(rows - 16, 16)], dst_ref=halo,
+            src_ref=tokens_hbm.at[pl.ds(rows - 16, 16)], dst_ref=halo,
             send_sem=halo_send.at[0], recv_sem=halo_recv.at[0],
             device_id=(group, target), device_id_type=MESH,
         )
@@ -292,6 +298,8 @@
 
     each(n, position, lambda other: filter_copy(other, position).start())
 
+    for load in loads[: len(early)]:
+        load.wait()
     gain = norm_gain[...].reshape(1, width)
     weight = in_weight[...]
 
@@ -317,7 +325,7 @@
     each(count, me, lambda other: signal_copy(other, me).start())
     signal[pl.ds(me, 1)] = sent[pl.ds(me, 1)]
 
-    for load in loads:
+    for load in loads[len(early) :]:
         load.wait()
     own_filter.wait()
     each(count, me, lambda other: signal_copy(me, other).wait_recv())
@@ -400,15 +408,17 @@
     first, last, second, turn = dft_tables(n, n * local_outer, rows, groups, share)
     low = jnp.bfloat16
     vmem = pl.BlockSpec(memory_space=pltpu.VMEM)
-    far = pl.BlockSpec(memory_space=pl.ANY)
+    far = pl.BlockSpec(memory_space=pltpu.HBM)
     dma = pltpu.SemaphoreType.DMA
+    small = [tokens, norm_gain, in_weight, short_filter, skip_gain, mlp_gain]
     held = [out_weight, up_weight, down_weight, first, last, second, turn]
     return pl.pallas_call(
         functools.partial(kernel, groups, n, share),
         out_shape=jax.ShapeDtypeStruct((rows, width), low),
-        in_specs=[vmem] * 6 + [far] * 8,
+        in_specs=[far] * 14,
         out_specs=vmem,
-        scratch_shapes=[
+        scratch_shapes=[pltpu.VMEM(a.shape, a.dtype) for a in small]
+        + [
             pltpu.VMEM((n, 2, share, local_outer, rows), low),
             pltpu.VMEM((16, width), low),
             pltpu.VMEM((rows + 8, 3 * width), jnp.float32),
@@ -419,11 +429,11 @@
         ]
         + [pltpu.VMEM(a.shape, a.dtype) for a in held]
         + [
-            dma((8,)), dma((n,)), dma((n,)), dma((1,)), dma((1,)),
+            dma((16,)), dma((n,)), dma((n,)), dma((1,)), dma((1,)),
             dma((count,)), dma((count,)), dma((count,)), dma((count,)),
         ],
         compiler_params=pltpu.CompilerParams(
-            collective_id=0, has_side_effects=True, vmem_limit_bytes=40 * 1024 * 1024
+            collective_id=0, has_side_effects=True, vmem_limit_bytes=64 * 1024 * 1024
         ),
     )(
         tokens, norm_gain, in_weight, short_filter, skip_gain, mlp_gain,

time: 42 us -> 30.6 us (0.73); the launches traced: 41.4 us -> 30.4 us
  local copies, waits for them, and re-layouts: 13.5 us -> 1.57 us
  Pallas kernels: 27.9 us -> 28.9 us
    unnamed x29 -> x1, local copies, waits for them, and re-layouts: 13.5 us -> 1.57 us
    pallas_call x1, Pallas kernels: 27.9 us -> 28.9 us  [fused(): pl.pallas_call(functools.partial(kernel, groups, n, share), out_shape=jax...]
where the time goes in v2:
time: 30.6 us; the launch traced here: 30.4 us
  Pallas kernels  28.9 us (94%)
  local copies, waits for them, and re-layouts  1.57 us (5%)
    pallas_call x1, Pallas kernels, fused(): pl.pallas_call(functools.partial(kernel, groups, n, share), out_shape=jax...  28.9 us
    unnamed x1, local copies, waits for them, and re-layouts  1.57 us

profile of v2, /device:TPU:0, one launch (start us, length us, event | category | flops | bytes accessed | tf_op | source)
XLA Modules:
  0.0 30.4 jit_solution(5090657100980874685)
XLA Ops:
  0.0 28.9 %shard_map.136 = bf16[256,256]{1,0:T(8,128)(2,1)} custom-call(bf16[256,256]{1,0:T(8,128)(2,1)} %tokens_hbm.1, f32[256]{0:T(256)} %norm_hbm.1, bf16[256,768]{1,0:T(8,128)(2,1)} %in_hbm.1, f32[3,768]{1,0:T(4,128)} %short_hbm.1, f32[256]{0:T(256)} %skip_hbm.1, f32[256]{0:T(256)} %mlp_hbm.1, bf16[2,256,2,256]{3,2,1,0:T(2,128)(2,1)} %spectra.1, ...), custom_call_target="tpu_custom_call" | custom-call | tf_op jit(solution)/shard_map/pallas_call | solution.py:415
  28.9 1.6 %copy.16 = bf16[256,256]{1,0:T(8,128)(2,1)} copy(bf16[256,256]{1,0:T(8,128)(2,1)} %shard_map.136) | data formatting | bytes 262144

commit v3 on v2

--- a/solution.py
+++ b/solution.py
@@ -225,7 +225,7 @@
         )
         return carry
 
-    lax.fori_loop(1, count, greet, 0)
+    lax.fori_loop(1, count, greet, 0, unroll=True)
 
     early = (
         (tokens_hbm, tokens), (norm_hbm, norm_gain), (in_hbm, in_weight),
@@ -251,7 +251,7 @@
     def filter_copy(target, source):
         return pltpu.make_async_remote_copy(
             src_ref=spectra.at[:, channels(target)], dst_ref=filt.at[source],
-            send_sem=filt_send.at[target], recv_sem=filt_recv.at[source],
+            send_sem=filt_send.at[0], recv_sem=filt_recv.at[0],
             device_id=(group, target), device_id_type=MESH,
         )
 
@@ -265,15 +265,22 @@
     def signal_copy(target, source):
         return pltpu.make_async_remote_copy(
             src_ref=sent.at[target], dst_ref=signal.at[source],
-            send_sem=sig_send.at[target], recv_sem=sig_recv.at[source],
+            send_sem=sig_send.at[0], recv_sem=sig_recv.at[0],
             device_id=place(target), device_id_type=MESH,
         )
 
     def response_copy(target, source):
         return pltpu.make_async_remote_copy(
             src_ref=back.at[target], dst_ref=response.at[source],
-            send_sem=resp_send.at[target], recv_sem=resp_recv.at[source],
+            send_sem=resp_send.at[0], recv_sem=resp_recv.at[0],
             device_id=place(target), device_id_type=MESH,
+        )
+
+    def all_of(landed, send_sem, recv_sem):
+        blocks = landed.at[pl.ds(0, landed.shape[0] - 1)]
+        return pltpu.make_async_remote_copy(
+            src_ref=blocks, dst_ref=blocks, send_sem=send_sem.at[0], recv_sem=recv_sem.at[0],
+            device_id=place(lax.rem(me + groups, count)), device_id_type=MESH,
         )
 
     def each(total, own, action):
@@ -281,7 +288,7 @@
             action(lax.rem(own + step, total))
             return carry
 
-        lax.fori_loop(1, total, body, 0)
+        lax.fori_loop(1, total, body, 0, unroll=True)
 
     for load in loads:
         load.start()
@@ -328,7 +335,7 @@
     for load in loads[len(early) :]:
         load.wait()
     own_filter.wait()
-    each(count, me, lambda other: signal_copy(me, other).wait_recv())
+    all_of(signal, sig_send, sig_recv).wait_recv()
 
     half = groups * n * share * (filt.shape[3])
     bins = half // groups
@@ -344,7 +351,7 @@
     spec = jnp.dot(turned, second[...], preferred_element_type=jnp.float32)
     spec_real = spec[:, :rows].reshape(groups, bins, rows)
     spec_imag = spec[:, rows:].reshape(groups, bins, rows)
-    each(n, position, lambda other: filter_copy(position, other).wait_recv())
+    all_of(filt, filt_send, filt_recv).wait_recv()
     filt_real = filt[:, 0].astype(jnp.float32).reshape(1, bins, rows)
     filt_imag = filt[:, 1].astype(jnp.float32).reshape(1, bins, rows)
     product = jnp.concatenate(
@@ -369,7 +376,7 @@
     back[...] = conv.reshape(count, share, rows).astype(jnp.bfloat16)
     each(count, me, lambda other: response_copy(other, me).start())
     response[pl.ds(me, 1)] = back[pl.ds(me, 1)]
-    each(count, me, lambda other: response_copy(me, other).wait_recv())
+    all_of(response, resp_send, resp_recv).wait_recv()
 
     answer = response[...].astype(jnp.float32).reshape(width, rows).T
     answer = answer + skip_gain[...].reshape(1, width) * driven
@@ -391,9 +398,9 @@
     def _():
         halo_copy(position + 1).wait_send()
 
-    each(n, position, lambda other: filter_copy(other, position).wait_send())
-    each(count, me, lambda other: signal_copy(other, me).wait_send())
-    each(count, me, lambda other: response_copy(other, me).wait_send())
+    all_of(filt, filt_send, filt_recv).wait_send()
+    all_of(signal, sig_send, sig_recv).wait_send()
+    all_of(response, resp_send, resp_recv).wait_send()
 
 
 def fused(
@@ -414,7 +421,7 @@
     held = [out_weight, up_weight, down_weight, first, last, second, turn]
     return pl.pallas_call(
         functools.partial(kernel, groups, n, share),
-        out_shape=jax.ShapeDtypeStruct((rows, width), low),
+        out_shape=pltpu.VMEM((rows, width), low),
         in_specs=[far] * 14,
         out_specs=vmem,
         scratch_shapes=[pltpu.VMEM(a.shape, a.dtype) for a in small]
@@ -429,11 +436,11 @@
         ]
         + [pltpu.VMEM(a.shape, a.dtype) for a in held]
         + [
-            dma((16,)), dma((n,)), dma((n,)), dma((1,)), dma((1,)),
-            dma((count,)), dma((count,)), dma((count,)), dma((count,)),
+            dma((16,)), dma((1,)), dma((1,)), dma((1,)), dma((1,)),
+            dma((1,)), dma((1,)), dma((1,)), dma((1,)),
         ],
         compiler_params=pltpu.CompilerParams(
-            collective_id=0, has_side_effects=True, vmem_limit_bytes=64 * 1024 * 1024
+            collective_id=0, has_side_effects=True, vmem_limit_bytes=56 * 1024 * 1024
         ),
     )(
         tokens, norm_gain, in_weight, short_filter, skip_gain, mlp_gain,

time: 30.6 us -> 26.6 us (0.87)
  Pallas kernels: 28.9 us -> 25.8 us
  local copies, waits for them, and re-layouts: 1.57 us -> 0.66 us
    pallas_call x1, Pallas kernels: 28.9 us -> 25.8 us  [fused(): pl.pallas_call(functools.partial(kernel, groups, n, share), out_shape=plt...]
    unnamed x1, local copies, waits for them, and re-layouts: 1.57 us -> 0.66 us
where the time goes in v3:
time: 26.6 us; the launch traced here: 26.4 us
  Pallas kernels  25.8 us (97%)
  local copies, waits for them, and re-layouts  0.66 us (2%)
    pallas_call x1, Pallas kernels, fused(): pl.pallas_call(functools.partial(kernel, groups, n, share), out_shape=plt...  25.8 us
    unnamed x1, local copies, waits for them, and re-layouts  0.66 us

profile of v3, /device:TPU:0, one launch (start us, length us, event | category | flops | bytes accessed | tf_op | source)
XLA Modules:
  0.0 26.4 jit_solution(16745311236331285048)
XLA Ops:
  0.0 25.8 %shard_map.136 = bf16[256,256]{1,0:T(8,128)(2,1)S(1)} custom-call(bf16[256,256]{1,0:T(8,128)(2,1)} %tokens_hbm.1, f32[256]{0:T(256)} %norm_hbm.1, bf16[256,768]{1,0:T(8,128)(2,1)} %in_hbm.1, f32[3,768]{1,0:T(4,128)} %short_hbm.1, f32[256]{0:T(256)} %skip_hbm.1, f32[256]{0:T(256)} %mlp_hbm.1, bf16[2,256,2,256]{3,2,1,0:T(2,128)(2,1)} %spectra.1, ...), custom_call_target="tpu_custom_call" | custom-call | tf_op jit(solution)/shard_map/pallas_call | solution.py:422
  25.8 0.7 %copy.16 = bf16[256,256]{1,0:T(8,128)(2,1)} copy(bf16[256,256]{1,0:T(8,128)(2,1)S(1)} %shard_map.136) | data formatting | bytes 262144

commit v4 on v3

--- a/solution.py
+++ b/solution.py
@@ -293,18 +293,6 @@
     for load in loads:
         load.start()
     own_filter.start()
-    pl.semaphore_wait(barrier, count - 1)
-
-    @pl.when(position < n - 1)
-    def _():
-        halo_copy(position + 1).start()
-
-    @pl.when(position == 0)
-    def _():
-        halo[...] = jnp.zeros_like(halo)
-
-    each(n, position, lambda other: filter_copy(other, position).start())
-
     for load in loads[: len(early)]:
         load.wait()
     gain = norm_gain[...].reshape(1, width)
@@ -316,6 +304,19 @@
         return made.astype(jnp.bfloat16).astype(jnp.float32)
 
     extended[pl.ds(8, rows), :] = project(tokens[...])
+
+    pl.semaphore_wait(barrier, count - 1)
+
+    @pl.when(position < n - 1)
+    def _():
+        halo_copy(position + 1).start()
+
+    @pl.when(position == 0)
+    def _():
+        halo[...] = jnp.zeros_like(halo)
+
+    for step in range(1, (n + 1) // 2):
+        filter_copy(lax.rem(position + step, n), position).start()
 
     @pl.when(position > 0)
     def _():
@@ -330,6 +331,8 @@
     driven = driven.astype(jnp.float32)
     sent[...] = driven.T.reshape(count, share, rows).astype(jnp.bfloat16)
     each(count, me, lambda other: signal_copy(other, me).start())
+    for step in range((n + 1) // 2, n):
+        filter_copy(lax.rem(position + step, n), position).start()
     signal[pl.ds(me, 1)] = sent[pl.ds(me, 1)]
 
     for load in loads[len(early) :]:

time: 26.6 us -> 26.1 us (0.981)
  Pallas kernels: 25.8 us -> 25.2 us
    pallas_call x1, Pallas kernels: 25.8 us -> 25.2 us  [fused(): pl.pallas_call(functools.partial(kernel, groups, n, share), out_shape=plt...]
where the time goes in v4:
time: 26.1 us; the launch traced here: 25.9 us
  Pallas kernels  25.2 us (97%)
  local copies, waits for them, and re-layouts  0.66 us (3%)
    pallas_call x1, Pallas kernels, fused(): pl.pallas_call(functools.partial(kernel, groups, n, share), out_shape=plt...  25.2 us
    unnamed x1, local copies, waits for them, and re-layouts  0.66 us

profile of v4, /device:TPU:0, one launch (start us, length us, event | category | flops | bytes accessed | tf_op | source)
XLA Modules:
  0.0 25.9 jit_solution(15730342036391263237)
XLA Ops:
  0.0 25.2 %shard_map.136 = bf16[256,256]{1,0:T(8,128)(2,1)S(1)} custom-call(bf16[256,256]{1,0:T(8,128)(2,1)} %tokens_hbm.1, f32[256]{0:T(256)} %norm_hbm.1, bf16[256,768]{1,0:T(8,128)(2,1)} %in_hbm.1, f32[3,768]{1,0:T(4,128)} %short_hbm.1, f32[256]{0:T(256)} %skip_hbm.1, f32[256]{0:T(256)} %mlp_hbm.1, bf16[2,256,2,256]{3,2,1,0:T(2,128)(2,1)} %spectra.1, ...), custom_call_target="tpu_custom_call" | custom-call | tf_op jit(solution)/shard_map/pallas_call | solution.py:425
  25.3 0.7 %copy.16 = bf16[256,256]{1,0:T(8,128)(2,1)} copy(bf16[256,256]{1,0:T(8,128)(2,1)S(1)} %shard_map.136) | data formatting | bytes 262144

commit v5 on v4

--- a/solution.py
+++ b/solution.py
@@ -305,6 +305,19 @@
 
     extended[pl.ds(8, rows), :] = project(tokens[...])
 
+    def drive(start, size):
+        mixed = short_filter[0:1, :] * extended[pl.ds(8 + start, size), :]
+        for lag in range(1, taps):
+            mixed = mixed + short_filter[lag : lag + 1, :] * extended[pl.ds(8 + start - lag, size), :]
+        query = mixed[:, :width].astype(jnp.bfloat16).astype(jnp.float32)
+        driven = (mixed[:, width : 2 * width] * mixed[:, 2 * width :]).astype(jnp.bfloat16)
+        driven = driven.astype(jnp.float32)
+        sent[:, :, pl.ds(start, size)] = driven.T.reshape(count, share, size).astype(jnp.bfloat16)
+        return query, driven
+
+    head = 128
+    query_tail, driven_tail = drive(head, rows - head)
+
     pl.semaphore_wait(barrier, count - 1)
 
     @pl.when(position < n - 1)
@@ -323,13 +336,9 @@
         halo_copy(position).wait_recv()
 
     extended[pl.ds(0, 8), :] = project(halo[...])[8:, :]
-    mixed = short_filter[0:1, :] * extended[pl.ds(8, rows), :]
-    for lag in range(1, taps):
-        mixed = mixed + short_filter[lag : lag + 1, :] * extended[pl.ds(8 - lag, rows), :]
-    query = mixed[:, :width].astype(jnp.bfloat16).astype(jnp.float32)
-    driven = (mixed[:, width : 2 * width] * mixed[:, 2 * width :]).astype(jnp.bfloat16)
-    driven = driven.astype(jnp.float32)
-    sent[...] = driven.T.reshape(count, share, rows).astype(jnp.bfloat16)
+    query_head, driven_head = drive(0, head)
+    query = jnp.concatenate([query_head, query_tail], axis=0)
+    driven = jnp.concatenate([driven_head, driven_tail], axis=0)
     each(count, me, lambda other: signal_copy(other, me).start())
     for step in range((n + 1) // 2, n):
         filter_copy(lax.rem(position + step, n), position).start()
@@ -474,6 +483,7 @@
             and rows == spectra.shape[3]
             and spectra.shape[2] == 2
             and rows % 128 == 0
+            and rows > 128
         )
         return (fused if fits else local)(*args)
 

time: 26.1 us -> 26.1 us (level)
  no operation moved by 1% of the time
where the time goes in v5:
time: 26.1 us; the launch traced here: 25.9 us
  Pallas kernels  25.2 us (97%)
  local copies, waits for them, and re-layouts  0.66 us (3%)
    pallas_call x1, Pallas kernels, fused(): pl.pallas_call(functools.partial(kernel, groups, n, share), out_shape=plt...  25.2 us
    unnamed x1, local copies, waits for them, and re-layouts  0.66 us

profile of v5, /device:TPU:0, one launch (start us, length us, event | category | flops | bytes accessed | tf_op | source)
XLA Modules:
  0.0 25.9 jit_solution(16311767975689340916)
XLA Ops:
  0.0 25.2 %shard_map.136 = bf16[256,256]{1,0:T(8,128)(2,1)S(1)} custom-call(bf16[256,256]{1,0:T(8,128)(2,1)} %tokens_hbm.1, f32[256]{0:T(256)} %norm_hbm.1, bf16[256,768]{1,0:T(8,128)(2,1)} %in_hbm.1, f32[3,768]{1,0:T(4,128)} %short_hbm.1, f32[256]{0:T(256)} %skip_hbm.1, f32[256]{0:T(256)} %mlp_hbm.1, bf16[2,256,2,256]{3,2,1,0:T(2,128)(2,1)} %spectra.1, ...), custom_call_target="tpu_custom_call" | custom-call | tf_op jit(solution)/shard_map/pallas_call | solution.py:434
  25.3 0.7 %copy.16 = bf16[256,256]{1,0:T(8,128)(2,1)} copy(bf16[256,256]{1,0:T(8,128)(2,1)S(1)} %shard_map.136) | data formatting | bytes 262144
